TPU v7x, 32 devices: a whole 2x2x4 slice. The times are simulated.
32 devices in a mesh: groups: 2 (over x), pairs: 16 (over z, y, core).
Axes of the slice: x: 2, y: 2, z: 4, core: 2. Of those that a mesh axis runs over, the one named last changes fastest.
Arguments:
- amplitudes: bfloat16 [2048, 128, 128], P(('groups', 'pairs')), parts along dimension 0, may hold values from -6 to 6
- pair_tiles: int32 [2048, 4], P('groups'), parts along dimension 0, may hold values from 0 to 31, as said below
- fit_vv: bfloat16 [24, 128, 16, 128], P('groups', 'pairs'), parts along dimension 0, as said below
- fit_ov: bfloat16 [64, 12, 16, 128], P(('groups', 'pairs')), parts along dimension 0, may hold values from -0.890625 to 0.890625
Outputs:
- residual: bfloat16 [2048, 128, 128], P(('groups', 'pairs')), parts along dimension 0
There are 2 independent parts, one for each index of `groups`. A program takes and returns all parts, laid end to end along the dimension named above; each array names one. Nothing has to cross between parts.
Inputs may be any that keep to these rules, and one draw needn't show every extreme that they name: `pair_tiles`: row r of the device s = r // 64 has k = s * 2 + r % 2. Column 1 is j, column 2 is A, column 3 is B; A and B are below 12. Among the rows of one device at most 4 have the same j // 2, and on every device some value of j // 2 is taken by exactly 4 rows. fit_vv[A, x, q, y] = fit_vv[A, y, q, x].
All inputs are finite; a program needn't handle non-finite values.
Results may differ from a plain program's by a relative error of at most 0.0049.
Values may be sent and summed in bfloat16 or wider, within the bound.
A program may use at most 128 MiB of HBM per device.

v0:
```python
import jax
import jax.numpy as jnp
from jax import lax
from jax.sharding import PartitionSpec as P


def body(amplitudes, pair_tiles, fit_vv, fit_ov):
    tiles_dev = amplitudes.shape[0]
    width = amplitudes.shape[1]
    devices_n = lax.axis_size("pairs")
    capacity = max(2, tiles_dev // devices_n)
    occ_dev = fit_ov.shape[0]
    vtiles = fit_ov.shape[1]
    fit_count = fit_ov.shape[2]
    here = lax.axis_index("pairs")
    mine = lax.dynamic_slice_in_dim(pair_tiles, here * tiles_dev, tiles_dev, 0)
    occ_k = mine[:, 0]
    occ_j = mine[:, 1]
    tile_a = mine[:, 2]
    tile_b = mine[:, 3]
    whole_vv = lax.all_gather(fit_vv, "pairs", axis=1, tiled=True)

    def ladder_block(step, ladder_acc):
        start = step * 8
        tiles_blk = lax.dynamic_slice_in_dim(amplitudes, start, 8, 0)
        left_ids = lax.dynamic_slice_in_dim(tile_a, start, 8, 0)
        right_ids = lax.dynamic_slice_in_dim(tile_b, start, 8, 0)
        left = jnp.take(whole_vv, left_ids, axis=0)
        right = jnp.take(whole_vv, right_ids, axis=0)
        inner = jnp.einsum(
            "pcd,pdqb->pcqb", tiles_blk, right, preferred_element_type=jnp.float32
        ).astype(jnp.bfloat16)
        block = jnp.einsum("paqc,pcqb->pab", left, inner, preferred_element_type=jnp.float32)
        return lax.dynamic_update_slice_in_dim(ladder_acc, block, start, 0)

    ladder = lax.fori_loop(
        0, tiles_dev // 8, ladder_block, jnp.zeros((tiles_dev, width, width), jnp.float32)
    )
    own_fit = fit_ov.reshape(occ_dev * vtiles, fit_count, width)
    fit_rows = jnp.take(own_fit, occ_k % occ_dev * vtiles + tile_a, axis=0)
    owners = jnp.arange(devices_n, dtype=jnp.int32)
    dest = occ_j // occ_dev
    hits = (dest[:, None] == owners[None, :]).astype(jnp.int32)
    rank = jnp.sum((jnp.cumsum(hits, axis=0) - 1) * hits, axis=1)
    slot = dest * capacity + rank
    every = pair_tiles.reshape(devices_n, tiles_dev, 4)
    to_here = (every[:, :, 1] // occ_dev == here).astype(jnp.int32)
    order_in = jnp.cumsum(to_here, axis=1) - 1
    slot_ids = jnp.arange(capacity, dtype=jnp.int32)
    picked = (
        to_here[:, :, None] * (order_in[:, :, None] == slot_ids[None, None, :]).astype(jnp.int32)
    ).astype(jnp.float32)
    column = every[:, :, 1] % occ_dev * vtiles + every[:, :, 3]
    columns_all = jnp.arange(occ_dev * vtiles, dtype=jnp.int32)
    column_hot = (column[:, :, None] == columns_all[None, None, :]).astype(jnp.float32)
    placing = jnp.einsum("spc,spm->scm", picked, column_hot, precision=lax.Precision.HIGHEST)
    placing = placing.reshape(devices_n * capacity, occ_dev * vtiles)
    payload = jnp.concatenate([amplitudes, fit_rows], axis=1)
    outgoing = (
        jnp.zeros((devices_n * capacity, width + fit_count, width), jnp.bfloat16)
        .at[slot]
        .set(payload)
    )
    incoming = lax.all_to_all(outgoing, "pairs", split_axis=0, concat_axis=0, tiled=True)
    got_tiles = incoming[:, :width]
    got_fit = incoming[:, width:]
    partial_value = jnp.einsum(
        "sqc,scb->sqb", got_fit, got_tiles, preferred_element_type=jnp.float32
    )
    totals = jnp.einsum("sm,sqb->mqb", placing, partial_value, precision=lax.Precision.HIGHEST)
    chosen = jnp.einsum("sm,mqb->sqb", placing, totals, precision=lax.Precision.HIGHEST)
    cycle_slots = jnp.einsum(
        "sqa,sqb->sab", got_fit.astype(jnp.float32), chosen, precision=lax.Precision.HIGHEST
    ).astype(jnp.bfloat16)
    returned = lax.all_to_all(cycle_slots, "pairs", split_axis=0, concat_axis=0, tiled=True)
    cycle = jnp.take(returned, slot, axis=0)
    cycle = lax.optimization_barrier(cycle)
    return (ladder + cycle.astype(jnp.float32)).astype(jnp.bfloat16)


def solution(mesh):
    in_specs = (
        P(("groups", "pairs"), None, None),
        P("groups", None),
        P("groups", "pairs", None, None),
        P(("groups", "pairs"), None, None, None),
    )
    out_specs = P(("groups", "pairs"), None, None)
    return jax.shard_map(body, mesh=mesh, in_specs=in_specs, out_specs=out_specs, check_vma=False)
```

profile of v0, /device:TPU:1, one launch (start us, length us, event | category | flops | bytes accessed | tf_op | source)
XLA Modules:
  0.0 403.4 jit_solution(5247963127664423122)
XLA Ops:
  12.7 9.0 %scatter_fusion = bf16[64,144,128]{2,1,0:T(8,128)(2,1)} fusion(bf16[64,144,128]{2,1,0:T(8,128)(2,1)} %broadcast_in_dim.45, s32[64]{0:T(128)S(1)} %bitcast.49, bf16[64,144,128]{2,1,0:T(8,128)(2,1)S(1)} %pad_maximum_fusion), kind=kCustom, calls=%fused_computation.4 | custom fusion | bytes 7078144 | tf_op jit(solution)/shard_map/scatter | solution.py:62
  21.7 7.4 %all-to-all-start = ((bf16[64,144,128]{2,1,0:T(8,128)(2,1)}), bf16[64,144,128]{2,1,0:T(8,128)(2,1)S(1)}, u32[]{:S(2)}, u32[]{:S(2)}) async-start(bf16[64,144,128]{2,1,0:T(8,128)(2,1)} %scatter_fusion), calls=%async_computation | async-start | bytes 4718592 | tf_op jit(solution)/shard_map/all_to_all | solution.py:64
  29.7 69.3 %all-to-all-done = bf16[64,144,128]{2,1,0:T(8,128)(2,1)S(1)} async-done(((bf16[64,144,128]{2,1,0:T(8,128)(2,1)}), bf16[64,144,128]{2,1,0:T(8,128)(2,1)S(1)}, u32[]{:S(2)}, u32[]{:S(2)}) %all-to-all-start) | async-done | bytes 2359328 | tf_op jit(solution)/shard_map/all_to_all | solution.py:64
  100.7 3.1 convolution_convert_fusion
  103.8 17.1 %all-to-all-start.1 = ((bf16[64,128,128]{2,1,0:T(8,128)(2,1)}), bf16[64,128,128]{2,1,0:T(8,128)(2,1)S(1)}, u32[]{:S(2)}, u32[]{:S(2)}) async-start(bf16[64,128,128]{2,1,0:T(8,128)(2,1)} %convolution_convert_fusion), calls=%async_computation.1 | async-start | bytes 4194304 | tf_op jit(solution)/shard_map/all_to_all | solution.py:75
  121.0 41.5 %all-to-all-done.1 = bf16[64,128,128]{2,1,0:T(8,128)(2,1)S(1)} async-done(((bf16[64,128,128]{2,1,0:T(8,128)(2,1)}), bf16[64,128,128]{2,1,0:T(8,128)(2,1)S(1)}, u32[]{:S(2)}, u32[]{:S(2)}) %all-to-all-start.1) | async-done | bytes 2097184 | tf_op jit(solution)/shard_map/all_to_all | solution.py:75
  168.9 223.4 %while.13 = (s32[]{:T(128)}, f32[64,128,128]{2,1,0:T(8,128)}, s32[64]{0:T(128)S(1)}, bf16[12,128,16,128]{3,2,1,0:T(8,128)(2,1)}, bf16[64,128,128]{2,1,0:T(8,128)...) while((s32[]{:T(128)}, f32[64,128,128]{2,1,0:T(8,128)}, s32[64]{0:T(128)S(1)}, ...), condition=%wide.region_1.3_spmd, body=%wide.region_0.2_spmd.sunk | while | flops 1080035456 | bytes 42739136 | solution.py:36
  169.0 5.9 %gather_fusion = bf16[8,128,16,128]{3,2,1,0:T(8,128)(2,1)} fusion(bf16[12,128,16,128]{3,2,1,0:T(8,128)(2,1)} %get-tuple-element.211, s32[1024]{0:T(1024)S(1)} %pad_clamp_fusion.6), kind=kCustom, calls=%fused_computation.1.clone.clone.1 | custom fusion | bytes 8388640 | tf_op jit(solution)/shard_map/while/body/eval_jaxpr/jit(_take)/gather | solution.py:29
  175.0 4.7 %broadcast_select_fusion.6 = bf16[8,128,16,128]{3,2,1,0:T(8,128)(2,1)} fusion(bf16[8,128,16,128]{3,2,1,0:T(8,128)(2,1)} %gather_fusion, pred[8]{0:T(512)(128)(4,1)S(1)} %get-tuple-element.185), kind=kLoop, calls=%fused_computation.10.clone.1 | loop fusion | flops 2097152 | bytes 8388616 | tf_op jit(solution)/shard_map/while/body/eval_jaxpr/jit(_take)/select_n | solution.py:29
  179.7 5.8 %gather_fusion.1 = bf16[8,128,16,128]{3,2,1,0:T(8,128)(2,1)} fusion(bf16[12,128,16,128]{3,2,1,0:T(8,128)(2,1)} %get-tuple-element.211, s32[1024]{0:T(1024)S(1)} %pad_clamp_fusion.7), kind=kCustom, calls=%fused_computation.clone.clone.1 | custom fusion | bytes 8388640 | tf_op jit(solution)/shard_map/while/body/eval_jaxpr/jit(_take)/gather | solution.py:28
  185.5 4.6 %broadcast_select_fusion.7 = bf16[8,128,16,128]{3,2,1,0:T(8,128)(2,1)} fusion(bf16[8,128,16,128]{3,2,1,0:T(8,128)(2,1)} %gather_fusion.1, pred[8]{0:T(512)(128)(4,1)S(1)} %get-tuple-element.187), kind=kLoop, calls=%fused_computation.11.clone.1 | loop fusion | flops 2097152 | bytes 8388616 | tf_op jit(solution)/shard_map/while/body/eval_jaxpr/jit(_take)/select_n | solution.py:28
  190.1 6.8 %fusion.67 = f32[64,128,128]{2,1,0:T(8,128)} fusion(f32[64,128,128]{2,1,0:T(8,128)} %get-tuple-element.199, s32[]{:T(128)S(6)} %select_n.125, bf16[8,128,16,128]{3,2,1,0:T(8,128)(2,1)} %broadcast_select_fusion.6, bf16[8,128,16,128]{3,2,1,0:T(8,128)(2,1)} %broadcast_select_fusion.7, bf16[64,128,128]{2,1,0:T(8,128)(2,1)} %get-tuple-element.212), kind=kOutput, calls=%fused_computation.13.clone.1 | convolution fusion | flops 1075838976 | bytes 9176064 | tf_op jit(solution)/shard_map/while/body/eval_jaxpr/paqc,pcqb->pab/dot_general | solution.py:33
  197.0 5.9 %gather_fusion = bf16[8,128,16,128]{3,2,1,0:T(8,128)(2,1)} fusion(bf16[12,128,16,128]{3,2,1,0:T(8,128)(2,1)} %get-tuple-element.211, s32[1024]{0:T(1024)S(1)} %pad_clamp_fusion.6), kind=kCustom, calls=%fused_computation.1.clone.clone.1 | custom fusion | bytes 8388640 | tf_op jit(solution)/shard_map/while/body/eval_jaxpr/jit(_take)/gather | solution.py:29
  202.9 4.7 %broadcast_select_fusion.6 = bf16[8,128,16,128]{3,2,1,0:T(8,128)(2,1)} fusion(bf16[8,128,16,128]{3,2,1,0:T(8,128)(2,1)} %gather_fusion, pred[8]{0:T(512)(128)(4,1)S(1)} %get-tuple-element.185), kind=kLoop, calls=%fused_computation.10.clone.1 | loop fusion | flops 2097152 | bytes 8388616 | tf_op jit(solution)/shard_map/while/body/eval_jaxpr/jit(_take)/select_n | solution.py:29
  207.6 5.8 %gather_fusion.1 = bf16[8,128,16,128]{3,2,1,0:T(8,128)(2,1)} fusion(bf16[12,128,16,128]{3,2,1,0:T(8,128)(2,1)} %get-tuple-element.211, s32[1024]{0:T(1024)S(1)} %pad_clamp_fusion.7), kind=kCustom, calls=%fused_computation.clone.clone.1 | custom fusion | bytes 8388640 | tf_op jit(solution)/shard_map/while/body/eval_jaxpr/jit(_take)/gather | solution.py:28
  213.5 4.6 %broadcast_select_fusion.7 = bf16[8,128,16,128]{3,2,1,0:T(8,128)(2,1)} fusion(bf16[8,128,16,128]{3,2,1,0:T(8,128)(2,1)} %gather_fusion.1, pred[8]{0:T(512)(128)(4,1)S(1)} %get-tuple-element.187), kind=kLoop, calls=%fused_computation.11.clone.1 | loop fusion | flops 2097152 | bytes 8388616 | tf_op jit(solution)/shard_map/while/body/eval_jaxpr/jit(_take)/select_n | solution.py:28
  218.1 6.7 %fusion.67 = f32[64,128,128]{2,1,0:T(8,128)} fusion(f32[64,128,128]{2,1,0:T(8,128)} %get-tuple-element.199, s32[]{:T(128)S(6)} %select_n.125, bf16[8,128,16,128]{3,2,1,0:T(8,128)(2,1)} %broadcast_select_fusion.6, bf16[8,128,16,128]{3,2,1,0:T(8,128)(2,1)} %broadcast_select_fusion.7, bf16[64,128,128]{2,1,0:T(8,128)(2,1)} %get-tuple-element.212), kind=kOutput, calls=%fused_computation.13.clone.1 | convolution fusion | flops 1075838976 | bytes 9176064 | tf_op jit(solution)/shard_map/while/body/eval_jaxpr/paqc,pcqb->pab/dot_general | solution.py:33
  224.9 5.9 %gather_fusion = bf16[8,128,16,128]{3,2,1,0:T(8,128)(2,1)} fusion(bf16[12,128,16,128]{3,2,1,0:T(8,128)(2,1)} %get-tuple-element.211, s32[1024]{0:T(1024)S(1)} %pad_clamp_fusion.6), kind=kCustom, calls=%fused_computation.1.clone.clone.1 | custom fusion | bytes 8388640 | tf_op jit(solution)/shard_map/while/body/eval_jaxpr/jit(_take)/gather | solution.py:29
  230.8 4.7 %broadcast_select_fusion.6 = bf16[8,128,16,128]{3,2,1,0:T(8,128)(2,1)} fusion(bf16[8,128,16,128]{3,2,1,0:T(8,128)(2,1)} %gather_fusion, pred[8]{0:T(512)(128)(4,1)S(1)} %get-tuple-element.185), kind=kLoop, calls=%fused_computation.10.clone.1 | loop fusion | flops 2097152 | bytes 8388616 | tf_op jit(solution)/shard_map/while/body/eval_jaxpr/jit(_take)/select_n | solution.py:29
  235.6 5.8 %gather_fusion.1 = bf16[8,128,16,128]{3,2,1,0:T(8,128)(2,1)} fusion(bf16[12,128,16,128]{3,2,1,0:T(8,128)(2,1)} %get-tuple-element.211, s32[1024]{0:T(1024)S(1)} %pad_clamp_fusion.7), kind=kCustom, calls=%fused_computation.clone.clone.1 | custom fusion | bytes 8388640 | tf_op jit(solution)/shard_map/while/body/eval_jaxpr/jit(_take)/gather | solution.py:28
  241.4 4.6 %broadcast_select_fusion.7 = bf16[8,128,16,128]{3,2,1,0:T(8,128)(2,1)} fusion(bf16[8,128,16,128]{3,2,1,0:T(8,128)(2,1)} %gather_fusion.1, pred[8]{0:T(512)(128)(4,1)S(1)} %get-tuple-element.187), kind=kLoop, calls=%fused_computation.11.clone.1 | loop fusion | flops 2097152 | bytes 8388616 | tf_op jit(solution)/shard_map/while/body/eval_jaxpr/jit(_take)/select_n | solution.py:28
  246.0 6.7 %fusion.67 = f32[64,128,128]{2,1,0:T(8,128)} fusion(f32[64,128,128]{2,1,0:T(8,128)} %get-tuple-element.199, s32[]{:T(128)S(6)} %select_n.125, bf16[8,128,16,128]{3,2,1,0:T(8,128)(2,1)} %broadcast_select_fusion.6, bf16[8,128,16,128]{3,2,1,0:T(8,128)(2,1)} %broadcast_select_fusion.7, bf16[64,128,128]{2,1,0:T(8,128)(2,1)} %get-tuple-element.212), kind=kOutput, calls=%fused_computation.13.clone.1 | convolution fusion | flops 1075838976 | bytes 9176064 | tf_op jit(solution)/shard_map/while/body/eval_jaxpr/paqc,pcqb->pab/dot_general | solution.py:33
  252.8 5.9 %gather_fusion = bf16[8,128,16,128]{3,2,1,0:T(8,128)(2,1)} fusion(bf16[12,128,16,128]{3,2,1,0:T(8,128)(2,1)} %get-tuple-element.211, s32[1024]{0:T(1024)S(1)} %pad_clamp_fusion.6), kind=kCustom, calls=%fused_computation.1.clone.clone.1 | custom fusion | bytes 8388640 | tf_op jit(solution)/shard_map/while/body/eval_jaxpr/jit(_take)/gather | solution.py:29
  258.7 4.7 %broadcast_select_fusion.6 = bf16[8,128,16,128]{3,2,1,0:T(8,128)(2,1)} fusion(bf16[8,128,16,128]{3,2,1,0:T(8,128)(2,1)} %gather_fusion, pred[8]{0:T(512)(128)(4,1)S(1)} %get-tuple-element.185), kind=kLoop, calls=%fused_computation.10.clone.1 | loop fusion | flops 2097152 | bytes 8388616 | tf_op jit(solution)/shard_map/while/body/eval_jaxpr/jit(_take)/select_n | solution.py:29
  263.5 5.8 %gather_fusion.1 = bf16[8,128,16,128]{3,2,1,0:T(8,128)(2,1)} fusion(bf16[12,128,16,128]{3,2,1,0:T(8,128)(2,1)} %get-tuple-element.211, s32[1024]{0:T(1024)S(1)} %pad_clamp_fusion.7), kind=kCustom, calls=%fused_computation.clone.clone.1 | custom fusion | bytes 8388640 | tf_op jit(solution)/shard_map/while/body/eval_jaxpr/jit(_take)/gather | solution.py:28
  269.3 4.6 %broadcast_select_fusion.7 = bf16[8,128,16,128]{3,2,1,0:T(8,128)(2,1)} fusion(bf16[8,128,16,128]{3,2,1,0:T(8,128)(2,1)} %gather_fusion.1, pred[8]{0:T(512)(128)(4,1)S(1)} %get-tuple-element.187), kind=kLoop, calls=%fused_computation.11.clone.1 | loop fusion | flops 2097152 | bytes 8388616 | tf_op jit(solution)/shard_map/while/body/eval_jaxpr/jit(_take)/select_n | solution.py:28
  273.9 6.8 %fusion.67 = f32[64,128,128]{2,1,0:T(8,128)} fusion(f32[64,128,128]{2,1,0:T(8,128)} %get-tuple-element.199, s32[]{:T(128)S(6)} %select_n.125, bf16[8,128,16,128]{3,2,1,0:T(8,128)(2,1)} %broadcast_select_fusion.6, bf16[8,128,16,128]{3,2,1,0:T(8,128)(2,1)} %broadcast_select_fusion.7, bf16[64,128,128]{2,1,0:T(8,128)(2,1)} %get-tuple-element.212), kind=kOutput, calls=%fused_computation.13.clone.1 | convolution fusion | flops 1075838976 | bytes 9176064 | tf_op jit(solution)/shard_map/while/body/eval_jaxpr/paqc,pcqb->pab/dot_general | solution.py:33
  280.7 5.9 %gather_fusion = bf16[8,128,16,128]{3,2,1,0:T(8,128)(2,1)} fusion(bf16[12,128,16,128]{3,2,1,0:T(8,128)(2,1)} %get-tuple-element.211, s32[1024]{0:T(1024)S(1)} %pad_clamp_fusion.6), kind=kCustom, calls=%fused_computation.1.clone.clone.1 | custom fusion | bytes 8388640 | tf_op jit(solution)/shard_map/while/body/eval_jaxpr/jit(_take)/gather | solution.py:29
  286.7 4.7 %broadcast_select_fusion.6 = bf16[8,128,16,128]{3,2,1,0:T(8,128)(2,1)} fusion(bf16[8,128,16,128]{3,2,1,0:T(8,128)(2,1)} %gather_fusion, pred[8]{0:T(512)(128)(4,1)S(1)} %get-tuple-element.185), kind=kLoop, calls=%fused_computation.10.clone.1 | loop fusion | flops 2097152 | bytes 8388616 | tf_op jit(solution)/shard_map/while/body/eval_jaxpr/jit(_take)/select_n | solution.py:29
  291.4 5.8 %gather_fusion.1 = bf16[8,128,16,128]{3,2,1,0:T(8,128)(2,1)} fusion(bf16[12,128,16,128]{3,2,1,0:T(8,128)(2,1)} %get-tuple-element.211, s32[1024]{0:T(1024)S(1)} %pad_clamp_fusion.7), kind=kCustom, calls=%fused_computation.clone.clone.1 | custom fusion | bytes 8388640 | tf_op jit(solution)/shard_map/while/body/eval_jaxpr/jit(_take)/gather | solution.py:28
  297.2 4.6 %broadcast_select_fusion.7 = bf16[8,128,16,128]{3,2,1,0:T(8,128)(2,1)} fusion(bf16[8,128,16,128]{3,2,1,0:T(8,128)(2,1)} %gather_fusion.1, pred[8]{0:T(512)(128)(4,1)S(1)} %get-tuple-element.187), kind=kLoop, calls=%fused_computation.11.clone.1 | loop fusion | flops 2097152 | bytes 8388616 | tf_op jit(solution)/shard_map/while/body/eval_jaxpr/jit(_take)/select_n | solution.py:28
  301.8 6.8 %fusion.67 = f32[64,128,128]{2,1,0:T(8,128)} fusion(f32[64,128,128]{2,1,0:T(8,128)} %get-tuple-element.199, s32[]{:T(128)S(6)} %select_n.125, bf16[8,128,16,128]{3,2,1,0:T(8,128)(2,1)} %broadcast_select_fusion.6, bf16[8,128,16,128]{3,2,1,0:T(8,128)(2,1)} %broadcast_select_fusion.7, bf16[64,128,128]{2,1,0:T(8,128)(2,1)} %get-tuple-element.212), kind=kOutput, calls=%fused_computation.13.clone.1 | convolution fusion | flops 1075838976 | bytes 9176064 | tf_op jit(solution)/shard_map/while/body/eval_jaxpr/paqc,pcqb->pab/dot_general | solution.py:33
  308.7 5.9 %gather_fusion = bf16[8,128,16,128]{3,2,1,0:T(8,128)(2,1)} fusion(bf16[12,128,16,128]{3,2,1,0:T(8,128)(2,1)} %get-tuple-element.211, s32[1024]{0:T(1024)S(1)} %pad_clamp_fusion.6), kind=kCustom, calls=%fused_computation.1.clone.clone.1 | custom fusion | bytes 8388640 | tf_op jit(solution)/shard_map/while/body/eval_jaxpr/jit(_take)/gather | solution.py:29
  314.7 4.7 %broadcast_select_fusion.6 = bf16[8,128,16,128]{3,2,1,0:T(8,128)(2,1)} fusion(bf16[8,128,16,128]{3,2,1,0:T(8,128)(2,1)} %gather_fusion, pred[8]{0:T(512)(128)(4,1)S(1)} %get-tuple-element.185), kind=kLoop, calls=%fused_computation.10.clone.1 | loop fusion | flops 2097152 | bytes 8388616 | tf_op jit(solution)/shard_map/while/body/eval_jaxpr/jit(_take)/select_n | solution.py:29
  319.4 5.8 %gather_fusion.1 = bf16[8,128,16,128]{3,2,1,0:T(8,128)(2,1)} fusion(bf16[12,128,16,128]{3,2,1,0:T(8,128)(2,1)} %get-tuple-element.211, s32[1024]{0:T(1024)S(1)} %pad_clamp_fusion.7), kind=kCustom, calls=%fused_computation.clone.clone.1 | custom fusion | bytes 8388640 | tf_op jit(solution)/shard_map/while/body/eval_jaxpr/jit(_take)/gather | solution.py:28
  325.2 4.6 %broadcast_select_fusion.7 = bf16[8,128,16,128]{3,2,1,0:T(8,128)(2,1)} fusion(bf16[8,128,16,128]{3,2,1,0:T(8,128)(2,1)} %gather_fusion.1, pred[8]{0:T(512)(128)(4,1)S(1)} %get-tuple-element.187), kind=kLoop, calls=%fused_computation.11.clone.1 | loop fusion | flops 2097152 | bytes 8388616 | tf_op jit(solution)/shard_map/while/body/eval_jaxpr/jit(_take)/select_n | solution.py:28
  329.8 6.8 %fusion.67 = f32[64,128,128]{2,1,0:T(8,128)} fusion(f32[64,128,128]{2,1,0:T(8,128)} %get-tuple-element.199, s32[]{:T(128)S(6)} %select_n.125, bf16[8,128,16,128]{3,2,1,0:T(8,128)(2,1)} %broadcast_select_fusion.6, bf16[8,128,16,128]{3,2,1,0:T(8,128)(2,1)} %broadcast_select_fusion.7, bf16[64,128,128]{2,1,0:T(8,128)(2,1)} %get-tuple-element.212), kind=kOutput, calls=%fused_computation.13.clone.1 | convolution fusion | flops 1075838976 | bytes 9176064 | tf_op jit(solution)/shard_map/while/body/eval_jaxpr/paqc,pcqb->pab/dot_general | solution.py:33
  336.7 5.9 %gather_fusion = bf16[8,128,16,128]{3,2,1,0:T(8,128)(2,1)} fusion(bf16[12,128,16,128]{3,2,1,0:T(8,128)(2,1)} %get-tuple-element.211, s32[1024]{0:T(1024)S(1)} %pad_clamp_fusion.6), kind=kCustom, calls=%fused_computation.1.clone.clone.1 | custom fusion | bytes 8388640 | tf_op jit(solution)/shard_map/while/body/eval_jaxpr/jit(_take)/gather | solution.py:29
  342.6 4.7 %broadcast_select_fusion.6 = bf16[8,128,16,128]{3,2,1,0:T(8,128)(2,1)} fusion(bf16[8,128,16,128]{3,2,1,0:T(8,128)(2,1)} %gather_fusion, pred[8]{0:T(512)(128)(4,1)S(1)} %get-tuple-element.185), kind=kLoop, calls=%fused_computation.10.clone.1 | loop fusion | flops 2097152 | bytes 8388616 | tf_op jit(solution)/shard_map/while/body/eval_jaxpr/jit(_take)/select_n | solution.py:29
  347.3 5.8 %gather_fusion.1 = bf16[8,128,16,128]{3,2,1,0:T(8,128)(2,1)} fusion(bf16[12,128,16,128]{3,2,1,0:T(8,128)(2,1)} %get-tuple-element.211, s32[1024]{0:T(1024)S(1)} %pad_clamp_fusion.7), kind=kCustom, calls=%fused_computation.clone.clone.1 | custom fusion | bytes 8388640 | tf_op jit(solution)/shard_map/while/body/eval_jaxpr/jit(_take)/gather | solution.py:28
  353.1 4.6 %broadcast_select_fusion.7 = bf16[8,128,16,128]{3,2,1,0:T(8,128)(2,1)} fusion(bf16[8,128,16,128]{3,2,1,0:T(8,128)(2,1)} %gather_fusion.1, pred[8]{0:T(512)(128)(4,1)S(1)} %get-tuple-element.187), kind=kLoop, calls=%fused_computation.11.clone.1 | loop fusion | flops 2097152 | bytes 8388616 | tf_op jit(solution)/shard_map/while/body/eval_jaxpr/jit(_take)/select_n | solution.py:28
  357.8 6.7 %fusion.67 = f32[64,128,128]{2,1,0:T(8,128)} fusion(f32[64,128,128]{2,1,0:T(8,128)} %get-tuple-element.199, s32[]{:T(128)S(6)} %select_n.125, bf16[8,128,16,128]{3,2,1,0:T(8,128)(2,1)} %broadcast_select_fusion.6, bf16[8,128,16,128]{3,2,1,0:T(8,128)(2,1)} %broadcast_select_fusion.7, bf16[64,128,128]{2,1,0:T(8,128)(2,1)} %get-tuple-element.212), kind=kOutput, calls=%fused_computation.13.clone.1 | convolution fusion | flops 1075838976 | bytes 9176064 | tf_op jit(solution)/shard_map/while/body/eval_jaxpr/paqc,pcqb->pab/dot_general | solution.py:33
  364.6 5.9 %gather_fusion = bf16[8,128,16,128]{3,2,1,0:T(8,128)(2,1)} fusion(bf16[12,128,16,128]{3,2,1,0:T(8,128)(2,1)} %get-tuple-element.211, s32[1024]{0:T(1024)S(1)} %pad_clamp_fusion.6), kind=kCustom, calls=%fused_computation.1.clone.clone.1 | custom fusion | bytes 8388640 | tf_op jit(solution)/shard_map/while/body/eval_jaxpr/jit(_take)/gather | solution.py:29
  370.5 4.7 %broadcast_select_fusion.6 = bf16[8,128,16,128]{3,2,1,0:T(8,128)(2,1)} fusion(bf16[8,128,16,128]{3,2,1,0:T(8,128)(2,1)} %gather_fusion, pred[8]{0:T(512)(128)(4,1)S(1)} %get-tuple-element.185), kind=kLoop, calls=%fused_computation.10.clone.1 | loop fusion | flops 2097152 | bytes 8388616 | tf_op jit(solution)/shard_map/while/body/eval_jaxpr/jit(_take)/select_n | solution.py:29
  375.2 5.8 %gather_fusion.1 = bf16[8,128,16,128]{3,2,1,0:T(8,128)(2,1)} fusion(bf16[12,128,16,128]{3,2,1,0:T(8,128)(2,1)} %get-tuple-element.211, s32[1024]{0:T(1024)S(1)} %pad_clamp_fusion.7), kind=kCustom, calls=%fused_computation.clone.clone.1 | custom fusion | bytes 8388640 | tf_op jit(solution)/shard_map/while/body/eval_jaxpr/jit(_take)/gather | solution.py:28
  381.1 4.6 %broadcast_select_fusion.7 = bf16[8,128,16,128]{3,2,1,0:T(8,128)(2,1)} fusion(bf16[8,128,16,128]{3,2,1,0:T(8,128)(2,1)} %gather_fusion.1, pred[8]{0:T(512)(128)(4,1)S(1)} %get-tuple-element.187), kind=kLoop, calls=%fused_computation.11.clone.1 | loop fusion | flops 2097152 | bytes 8388616 | tf_op jit(solution)/shard_map/while/body/eval_jaxpr/jit(_take)/select_n | solution.py:28
  385.7 6.7 %fusion.67 = f32[64,128,128]{2,1,0:T(8,128)} fusion(f32[64,128,128]{2,1,0:T(8,128)} %get-tuple-element.199, s32[]{:T(128)S(6)} %select_n.125, bf16[8,128,16,128]{3,2,1,0:T(8,128)(2,1)} %broadcast_select_fusion.6, bf16[8,128,16,128]{3,2,1,0:T(8,128)(2,1)} %broadcast_select_fusion.7, bf16[64,128,128]{2,1,0:T(8,128)(2,1)} %get-tuple-element.212), kind=kOutput, calls=%fused_computation.13.clone.1 | convolution fusion | flops 1075838976 | bytes 9176064 | tf_op jit(solution)/shard_map/while/body/eval_jaxpr/paqc,pcqb->pab/dot_general | solution.py:33
  392.4 4.1 %add_convert_fusion = bf16[64,128,128]{2,1,0:T(8,128)(2,1)} fusion(f32[64,128,128]{2,1,0:T(8,128)} %get-tuple-element.115, bf16[64,128,128]{2,1,0:T(8,128)(2,1)S(1)} %broadcast_select_fusion.2), kind=kLoop, calls=%fused_computation.23 | loop fusion | flops 3145728 | bytes 8388608 | tf_op jit(solution)/shard_map/convert_element_type | solution.py:78
  (56 shorter events, 15.7 us)
Async XLA Ops:
  6.5 1.7 copy-start
  6.5 159.9 %all-gather.2.cloned.1.call-start = ((), (), s32[]{:S(2)}) async-start(), calls=%async_computation.2 | async-start | bytes 6684672 | tf_op jit(solution)/shard_map/all_gather | solution.py:21
  12.7 16.3 %copy-start.1 = (s32[1024,4]{0,1:T(4,128)S(1)}, s32[1024,4]{0,1:T(4,128)}, u32[]{:S(2)}) copy-start(s32[1024,4]{0,1:T(4,128)} %param.9) | copy-start | bytes 49156
  21.7 77.3 %all-to-all-start = ((bf16[64,144,128]{2,1,0:T(8,128)(2,1)}), bf16[64,144,128]{2,1,0:T(8,128)(2,1)S(1)}, u32[]{:S(2)}, u32[]{:S(2)}) async-start(bf16[64,144,128]{2,1,0:T(8,128)(2,1)} %scatter_fusion), calls=%async_computation | async-start | bytes 4718592 | tf_op jit(solution)/shard_map/all_to_all | solution.py:64
  103.8 58.6 %all-to-all-start.1 = ((bf16[64,128,128]{2,1,0:T(8,128)(2,1)}), bf16[64,128,128]{2,1,0:T(8,128)(2,1)S(1)}, u32[]{:S(2)}, u32[]{:S(2)}) async-start(bf16[64,128,128]{2,1,0:T(8,128)(2,1)} %convolution_convert_fusion), calls=%async_computation.1 | async-start | bytes 4194304 | tf_op jit(solution)/shard_map/all_to_all | solution.py:75
Sparse Core Ops, SparseCore 0:
  9.5 99.5 all-gather.1
where the time goes:
time: 411 us; the launch traced here: 403 us
  local copies, waits for them, and re-layouts  111 us (27%)
  waiting for transfers between devices  111 us (27%)
  other arithmetic  83.8 us (20%)
  matrix products  59.1 us (14%)
  starting transfers between devices  24.5 us (6%)
  between operations  13.5 us (3%)
    all_to_all x1, waiting for transfers between devices, body(): lax.all_to_all(outgoing, 'pairs', split_axis=0, concat_axis=0, tiled=True)  69.3 us
    dot_general x8, matrix products, ladder_block(): jnp.einsum('paqc,pcqb->pab', left, inner, preferred_element_type=jnp.floa...  54 us
    gather x8, local copies, waits for them, and re-layouts, ladder_block(): right = jnp.take(whole_vv, right_ids, axis=0)  47.5 us
    gather x8, local copies, waits for them, and re-layouts, ladder_block(): left = jnp.take(whole_vv, left_ids, axis=0)  46.5 us
    all_to_all x1, waiting for transfers between devices, body(): lax.all_to_all(cycle_slots, 'pairs', split_axis=0, concat_axis=0, tiled=T...  41.5 us
    select_n x8, other arithmetic, ladder_block(): right = jnp.take(whole_vv, right_ids, axis=0)  37.8 us
    select_n x8, other arithmetic, ladder_block(): left = jnp.take(whole_vv, left_ids, axis=0)  36.8 us
    all_to_all x1, starting transfers between devices, body(): lax.all_to_all(cycle_slots, 'pairs', split_axis=0, concat_axis=0, tiled=T...  17.1 us
  transfers between devices with their start and end apart: 3, of which 2 were waited for; matrix products, arithmetic and copies ran while one was open for 6% of the time, Pallas kernels for 0%

commit v1 on v0

v1 whole, which is shorter than its diff:
```python
import functools

import jax
import jax.numpy as jnp
from jax import lax
from jax.experimental import pallas as pl
from jax.experimental.pallas import tpu as pltpu
from jax.sharding import PartitionSpec as P

F32 = jnp.float32
BF16 = jnp.bfloat16


def grid_of(n):
    ny = 2 if n == 16 else 1
    return n // (2 * ny), ny


def comm_kernel(
    n, cap, fit_count,
    perm_ref, row_ref, vv_ref, amp_ref, fit_ref, code_col_ref, code_row_ref,
    v_ref, chosen_ref,
    gbuf, part, inbuf, back,
    send_sem, recv_sem, go_send, go_recv, ret_send, ret_recv,
):
    nz, ny = grid_of(n)
    me = lax.axis_index("pairs")
    z, y, c = me // (2 * ny), (me // 2) % ny, me % 2
    vtiles, rows_dev = vv_ref.shape[0], vv_ref.shape[1]
    block = cap * fit_count

    def index(zz, yy, cc):
        return (zz * ny + yy) * 2 + cc

    barrier = pltpu.get_barrier_semaphore()
    for off in range(1, n):
        pl.semaphore_signal(barrier, inc=1, device_id={"pairs": (me + off) % n},
                            device_id_type=pl.DeviceIdType.MESH)
    pl.semaphore_wait(barrier, n - 1)

    def remote(src, dst, ssem, rsem, dev):
        return pltpu.make_async_remote_copy(
            src_ref=src, dst_ref=dst, send_sem=ssem, recv_sem=rsem,
            device_id={"pairs": dev}, device_id_type=pl.DeviceIdType.MESH)

    started = []

    def send(src, shard, dev, cond):
        k = len(started)
        cp = remote(src, gbuf.at[shard], send_sem.at[k], recv_sem.at[shard], dev)
        started.append((cp, cond))
        if cond is None:
            cp.start()
        else:
            pl.when(cond)(cp.start)

    def arrived(shard, cond=None):
        cp = remote(gbuf.at[shard], gbuf.at[shard], send_sem.at[0], recv_sem.at[shard], me)
        if cond is None:
            cp.wait_recv()
        else:
            pl.when(cond)(cp.wait_recv)

    up_ok, down_ok = z + 1 < nz, z >= 1
    up, down = jnp.minimum(z + 1, nz - 1), jnp.maximum(z - 1, 0)
    send(vv_ref, me, index(up, y, c), up_ok)
    send(vv_ref, me, index(down, y, c), down_ok)
    if ny == 2:
        send(vv_ref, me, index(z, 1 - y, c), None)
    send(vv_ref, me, index(z, y, 1 - c), None)

    def one_partial(s, carry):
        p = perm_ref[s]
        val = jnp.dot(fit_ref[row_ref[s]], amp_ref[p], preferred_element_type=F32)
        part[pl.ds(pl.multiple_of(s * fit_count, fit_count), fit_count), :] = val.astype(BF16)
        return carry

    lax.fori_loop(0, n * cap, one_partial, 0, unroll=4)

    def slab(ref, i):
        return ref.at[pl.ds(pl.multiple_of(i * block, block), block)]

    go = []
    for off in range(1, n):
        dev = (me + off) % n
        cp = remote(slab(part, dev), slab(inbuf, me), go_send.at[off], go_recv.at[off], dev)
        cp.start()
        go.append(cp)
    here = pl.ds(pl.multiple_of(me * block, block), block)
    inbuf[here, :] = part[here, :]

    def z_step(k):
        for zz, okay, nxt, nxt_ok in ((z - k, z >= k, up, up_ok), (z + k, z + k < nz, down, down_ok)):
            zs = jnp.clip(zz, 0, nz - 1)
            shard = index(zs, y, c)
            arrived(shard, okay)
            src = gbuf.at[shard]
            send(src, shard, index(nxt, y, c), jnp.logical_and(okay, nxt_ok))
            if ny == 2:
                send(src, shard, index(z, 1 - y, c), okay)
            send(src, shard, index(z, y, 1 - c), okay)

    z_step(1)

    for cp in go:
        cp.wait_recv()
    total_rows = n * block
    mt = 256
    code_row = code_row_ref[...]
    values = inbuf[...]

    def totals(i, carry):
        r = pl.ds(pl.multiple_of(i * mt, mt), mt)
        same = jnp.where(code_col_ref[r, :] == code_row, 1.0, 0.0).astype(BF16)
        back[r, :] = jnp.dot(same, values, preferred_element_type=F32).astype(BF16)
        return carry

    lax.fori_loop(0, total_rows // mt, totals, 0)
    ret = []
    for off in range(1, n):
        dev = (me + off) % n
        cp = remote(slab(back, dev), slab(chosen_ref, me), ret_send.at[off], ret_recv.at[off], dev)
        cp.start()
        ret.append(cp)
    chosen_ref[here, :] = back[here, :]

    for k in range(2, nz):
        z_step(k)

    def relayout(lo, hi, m):
        if rows_dev != 8:
            return

        def one(i, carry):
            a0 = lo[i].astype(F32)
            a1 = hi[i].astype(F32)
            rows = pl.ds(pl.multiple_of(m * 16, 16), 16)
            for h in range(rows_dev):
                for e in range(2):
                    both = jnp.concatenate(
                        [a0[h, 8 * e:8 * e + 8], a1[h, 8 * e:8 * e + 8]], axis=0)
                    v_ref[i, 2 * h + e, rows, :] = both.astype(BF16)
            return carry

        lax.fori_loop(0, vtiles, one, 0)

    def chip(zz, yy):
        base = index(zz, yy, 0)
        relayout(gbuf.at[base], gbuf.at[base + 1], base // 2)

    gbuf[me] = vv_ref[...]
    for k in range(nz):
        zz = (z + k) % nz
        arrived(index(zz, y, 1 - c))
        chip(zz, y)
    if ny == 2:
        order = [(z, None)]
        for k in range(1, nz):
            order += [(z - k, z >= k), (z + k, z + k < nz)]
        for zz, cond in order:
            shard = index(jnp.clip(zz, 0, nz - 1), 1 - y, c)
            arrived(shard, cond)
            send(gbuf.at[shard], shard, index(z, y, 1 - c), cond)
        for zz, cond in order:
            zc = jnp.clip(zz, 0, nz - 1)

            def finish(zc=zc):
                arrived(index(zc, 1 - y, 1 - c))
                chip(zc, 1 - y)

            if cond is None:
                finish()
            else:
                pl.when(cond)(finish)
    if rows_dev != 8:
        for i in range(n):
            v_ref[:, i * rows_dev:(i + 1) * rows_dev] = gbuf[i]
    for cp in ret:
        cp.wait_recv()
    for cp in go + ret:
        cp.wait_send()
    for cp, cond in started:
        if cond is None:
            cp.wait_send()
        else:
            pl.when(cond)(cp.wait_send)


def ladder_kernel(a_ids, b_ids, fit_ids, slots, v_ref, amp_ref, fit_ref, chosen_ref, out_ref):
    tiles = amp_ref.shape[0]
    q_count = v_ref.shape[1]
    width = v_ref.shape[2]

    def one(p, carry):
        left, right = v_ref[a_ids[p]], v_ref[b_ids[p]]
        wide = jnp.concatenate([right[q] for q in range(q_count)], axis=1)
        inner = jnp.dot(amp_ref[p], wide, preferred_element_type=F32).astype(BF16)
        tall = jnp.concatenate(
            [inner[:, q * width:(q + 1) * width] for q in range(q_count)], axis=0)
        acc = jnp.dot(
            jnp.concatenate([left[q] for q in range(q_count)], axis=1), tall,
            preferred_element_type=F32)
        cyc = lax.dot_general(
            fit_ref[fit_ids[p]], chosen_ref[slots[p]], (((0,), (0,)), ((), ())),
            preferred_element_type=F32).astype(BF16)
        out_ref[p] = (acc + cyc.astype(F32)).astype(BF16)
        return carry

    lax.fori_loop(0, tiles, one, 0, unroll=2)


def body(amplitudes, pair_tiles, fit_vv, fit_ov):
    tiles_dev, width = amplitudes.shape[0], amplitudes.shape[1]
    n = lax.axis_size("pairs")
    cap = max(2, tiles_dev // n)
    slots_n = n * cap
    occ_dev, vtiles, fit_count = fit_ov.shape[0], fit_ov.shape[1], fit_ov.shape[2]
    rows_dev = fit_vv.shape[1]
    here = lax.axis_index("pairs")
    mine = lax.dynamic_slice_in_dim(pair_tiles, here * tiles_dev, tiles_dev, 0)
    tile_a, tile_b = mine[:, 2], mine[:, 3]
    dest = mine[:, 1] // occ_dev
    fit_ids = mine[:, 0] % occ_dev * vtiles + tile_a
    steps = jnp.arange(tiles_dev, dtype=jnp.int32)
    earlier = steps[None, :] < steps[:, None]
    rank = jnp.sum(((dest[:, None] == dest[None, :]) & earlier).astype(jnp.int32), axis=1)
    slot = dest * cap + rank
    hit = (slot[None, :] == jnp.arange(slots_n, dtype=jnp.int32)[:, None]).astype(jnp.int32)
    perm = jnp.sum(hit * steps[None, :], axis=1)
    slot_fit = jnp.sum(hit * fit_ids[None, :], axis=1)

    every = pair_tiles.reshape(n, tiles_dev, 4)
    to_here = every[:, :, 1] // occ_dev == here
    order_in = jnp.sum((to_here[:, None, :] & earlier[None]).astype(jnp.int32), axis=2)
    column = every[:, :, 1] % occ_dev * vtiles + every[:, :, 3]
    picked = to_here[:, :, None] & (order_in[:, :, None] == jnp.arange(cap, dtype=jnp.int32))
    code = jnp.sum(jnp.where(picked, column[:, :, None] + 1, 0), axis=1) - 1
    code = code.reshape(slots_n, 1) * fit_count + jnp.arange(fit_count, dtype=jnp.int32)[None, :]
    code = code.reshape(slots_n * fit_count)

    own = fit_vv
    if rows_dev == 8:
        own = jnp.transpose(fit_vv, (0, 2, 1, 3)).reshape(vtiles, rows_dev, 16, width)
    fits = fit_ov.reshape(occ_dev * vtiles, fit_count, width)

    vmem = pl.BlockSpec(memory_space=pltpu.VMEM)
    smem = pl.BlockSpec(memory_space=pltpu.SMEM)
    nz, ny = grid_of(n)
    sends = 4 + 6 * (nz - 1) + 2 * nz
    dma = pltpu.SemaphoreType.DMA
    v_shape = (vtiles, fit_count, width, width) if rows_dev == 8 else (vtiles, width, fit_count, width)
    flat = (slots_n * fit_count, width)
    whole, chosen = pl.pallas_call(
        functools.partial(comm_kernel, n, cap, fit_count),
        out_shape=(jax.ShapeDtypeStruct(v_shape, BF16), jax.ShapeDtypeStruct(flat, BF16)),
        in_specs=[smem, smem, vmem, vmem, vmem, vmem, vmem],
        out_specs=(vmem, vmem),
        scratch_shapes=[
            pltpu.VMEM((n, vtiles, rows_dev, 16, width), BF16),
            pltpu.VMEM(flat, BF16),
            pltpu.VMEM(flat, BF16),
            pltpu.VMEM(flat, BF16),
            dma((sends,)),
            dma((n,)),
            dma((n,)),
            dma((n,)),
            dma((n,)),
            dma((n,)),
        ],
        compiler_params=pltpu.CompilerParams(
            collective_id=0, has_side_effects=True, vmem_limit_bytes=48 * 2**20),
        name="gather_and_totals",
    )(perm, slot_fit, own, amplitudes, fits, code[:, None], code[None, :])
    if rows_dev != 8:
        whole = jnp.transpose(whole, (0, 2, 1, 3))
    chosen = chosen.reshape(slots_n, fit_count, width)
    flops = 4 * tiles_dev * fit_count * width**3
    return pl.pallas_call(
        ladder_kernel,
        out_shape=jax.ShapeDtypeStruct(amplitudes.shape, BF16),
        in_specs=[smem, smem, smem, smem, vmem, vmem, vmem, vmem],
        out_specs=vmem,
        compiler_params=pltpu.CompilerParams(vmem_limit_bytes=48 * 2**20),
        cost_estimate=pl.CostEstimate(flops=flops, bytes_accessed=12 * 2**20, transcendentals=0),
        name="ladder",
    )(tile_a, tile_b, fit_ids, slot, whole, amplitudes, fits, chosen)


def solution(mesh):
    in_specs = (
        P(("groups", "pairs"), None, None),
        P("groups", None),
        P("groups", "pairs", None, None),
        P(("groups", "pairs"), None, None, None),
    )
    out_specs = P(("groups", "pairs"), None, None)
    return jax.shard_map(body, mesh=mesh, in_specs=in_specs, out_specs=out_specs, check_vma=False)
```

time: 411 us -> 91.9 us (0.22); the launches traced: 403 us -> 91.6 us
  waiting for transfers between devices: 111 us -> 0 us
  local copies, waits for them, and re-layouts: 111 us -> 5.71 us
  Pallas kernels: 0 us -> 84.9 us
  other arithmetic: 83.8 us -> 0.95 us
  matrix products: 59.1 us -> 0 us
  starting transfers between devices: 24.5 us -> 0 us
  between operations: 13.5 us -> 0.1 us
    all_to_all x2 -> x0, waiting for transfers between devices: 111 us -> none  [the longest x1 69.3 us: body(): lax.all_to_all(outgoing, 'pairs', split_axis=0, concat_axis=0, tiled=True)]
    gather x18 -> x0, local copies, waits for them, and re-layouts: 96.9 us -> none  [the longest x8 47.5 us: ladder_block(): right = jnp.take(whole_vv, right_ids, axis=0)]
    pallas_call x0 -> x2, Pallas kernels: none -> 84.9 us  [the longest x1 57.4 us: body(): pl.pallas_call(functools.partial(comm_kernel, n, cap, fit_count), out_sha...]
    select_n x19 -> x1, other arithmetic: 76.6 us -> 0.01 us  [body(): dest = mine[:, 1] // occ_dev]
    dot_general x13 -> x0, matrix products: 59.1 us -> none  [the longest x8 54 us: ladder_block(): jnp.einsum('paqc,pcqb->pab', left, inner, preferred_element_type=jnp.floa...]
    all_to_all x2 -> x0, starting transfers between devices: 24.5 us -> none  [the longest x1 17.1 us: body(): lax.all_to_all(cycle_slots, 'pairs', split_axis=0, concat_axis=0, tiled=T...]
    scatter x1 -> x0, local copies, waits for them, and re-layouts: 8.99 us -> none  [body(): outgoing = jnp.zeros((devices_n * capacity, width + fit_count, width), jn...]
    broadcast_in_dim x2 -> x0, local copies, waits for them, and re-layouts: 4.26 us -> none  [the longest x1 2.53 us: body(): jnp.zeros((tiles_dev, width, width), jnp.float32)]
  transfers between devices with their start and end apart: 3 -> 0, of which waited for: 2 -> 0; matrix products, arithmetic and copies ran while one was open for 6% -> 0% of each run, Pallas kernels for 0% -> 0%
where the time goes in v1:
time: 91.9 us; the launch traced here: 91.6 us
  Pallas kernels  84.9 us (92%)
  local copies, waits for them, and re-layouts  5.71 us (6%)
  other arithmetic  0.95 us (1%)
    pallas_call x1, Pallas kernels, body(): pl.pallas_call(functools.partial(comm_kernel, n, cap, fit_count), out_sha...  57.4 us
    pallas_call x1, Pallas kernels, body(): pl.pallas_call(ladder_kernel, out_shape=jax.ShapeDtypeStruct(amplitudes.s...  27.4 us
    unnamed x6, local copies, waits for them, and re-layouts  2.48 us

profile of v1, /device:TPU:1, one launch (start us, length us, event | category | flops | bytes accessed | tf_op | source)
XLA Modules:
  0.0 91.6 jit_solution(15994266005124236326)
XLA Ops:
  0.0 0.8 constant_dynamic-slice_fusion
  0.8 0.2 convert_reduce_fusion.1
  1.0 0.1 select_reduce_fusion.1
  1.1 0.8 reshape.183
  1.9 0.4 convert_reduce_fusion
  2.3 0.1 select_reduce_fusion
  2.5 0.1 copy.9
  2.6 0.1 mul.70
  2.7 0.1 iota_add_fusion
  2.7 0.1 add.102.code_row_ref
  2.8 1.1 %copy.8 = bf16[12,16,8,128]{3,2,1,0:T(8,128)(2,1)S(1)} copy(bf16[12,16,8,128]{3,1,2,0:T(8,128)(2,1)} %bitcast.48) | data formatting | bytes 786432 | tf_op jit(solution)/shard_map/transpose | solution.py:243
  3.9 0.3 add.103.code_col_ref
  4.2 0.0 copy-start
  4.3 1.6 %copy-done = bf16[64,128,128]{2,1,0:T(8,128)(2,1)S(1)} copy-done((bf16[64,128,128]{2,1,0:T(8,128)(2,1)S(1)}, bf16[64,128,128]{2,1,0:T(8,128)(2,1)}, u32[]{:S(2)}) %copy-start) | copy-done | bytes 2097176
  5.8 0.0 copy-start.2
  5.8 0.9 copy-done.2
  6.7 0.0 copy-start.1
  6.7 57.4 %gather_and_totals.1 = (bf16[12,16,128,128]{3,2,1,0:T(8,128)(2,1)}, bf16[1024,128]{1,0:T(8,128)(2,1)S(1)}) custom-call(s32[64]{0:T(128)S(1)} %get-tuple-element.10.perm_ref, s32[64]{0:T(128)S(1)} %get-tuple-element.9.row_ref, bf16[12,8,16,128]{3,2,1,0:T(8,128)(2,1)S(1)} %bitcast.44, bf16[64,128,128]{2,1,0:T(8,128)(2,1)S(1)} %copy-done, ...), custom_call_target="tpu_custom_call" | custom-call | tf_op jit(solution)/shard_map/gather_and_totals/pallas_call | solution.py:253
  64.2 0.0 copy-done.1
  64.2 27.4 %ladder.1 = bf16[64,128,128]{2,1,0:T(8,128)(2,1)} custom-call(s32[64]{0:T(128)S(1)} %get-tuple-element.15.a_ids, s32[64]{0:T(128)S(1)} %get-tuple-element.14.b_ids, s32[64]{0:T(128)S(1)} %get-tuple-element.17.fit_ids, s32[64]{0:T(128)S(1)} %multiply_add_fusion.slots, bf16[12,16,128,128]{3,2,1,0:T(8,128)(2,1)} %get-tuple-element.7.v_ref, ...), custom_call_target="tpu_custom_call" | custom-call | flops 8589934592 | bytes 12582912 | tf_op jit(solution)/shard_map/ladder/pallas_call | solution.py:278
  (8 shorter events, 0.1 us)
Async XLA Ops:
  4.2 1.6 %copy-start = (bf16[64,128,128]{2,1,0:T(8,128)(2,1)S(1)}, bf16[64,128,128]{2,1,0:T(8,128)(2,1)}, u32[]{:S(2)}) copy-start(bf16[64,128,128]{2,1,0:T(8,128)(2,1)} %amp_ref.3) | copy-start | bytes 6291460
  5.8 0.9 copy-start.2
  6.7 57.4 %copy-start.1 = (bf16[64,128,128]{2,1,0:T(8,128)(2,1)S(1)}, bf16[64,128,128]{2,1,0:T(8,128)(2,1)}, u32[]{:S(2)}) copy-start(bf16[64,128,128]{2,1,0:T(8,128)(2,1)} %amp_ref.3) | copy-start | bytes 6291460

commit v2 on v1

--- a/solution.py
+++ b/solution.py
@@ -9,6 +9,9 @@
 
 F32 = jnp.float32
 BF16 = jnp.bfloat16
+
+
+CHUNKS = 4
 
 
 def grid_of(n):
@@ -45,17 +48,22 @@
 
     started = []
 
-    def send(src, shard, dev, cond):
+    per = vtiles // CHUNKS
+
+    def send(src, shard, h, dev, cond):
         k = len(started)
-        cp = remote(src, gbuf.at[shard], send_sem.at[k], recv_sem.at[shard], dev)
+        part_of = pl.ds(h * per, per)
+        cp = remote(src.at[part_of], gbuf.at[shard, part_of], send_sem.at[k],
+                    recv_sem.at[shard * CHUNKS + h], dev)
         started.append((cp, cond))
         if cond is None:
             cp.start()
         else:
             pl.when(cond)(cp.start)
 
-    def arrived(shard, cond=None):
-        cp = remote(gbuf.at[shard], gbuf.at[shard], send_sem.at[0], recv_sem.at[shard], me)
+    def arrived(shard, h, cond=None):
+        ref = gbuf.at[shard, pl.ds(h * per, per)]
+        cp = remote(ref, ref, send_sem.at[0], recv_sem.at[shard * CHUNKS + h], me)
         if cond is None:
             cp.wait_recv()
         else:
@@ -63,11 +71,12 @@
 
     up_ok, down_ok = z + 1 < nz, z >= 1
     up, down = jnp.minimum(z + 1, nz - 1), jnp.maximum(z - 1, 0)
-    send(vv_ref, me, index(up, y, c), up_ok)
-    send(vv_ref, me, index(down, y, c), down_ok)
-    if ny == 2:
-        send(vv_ref, me, index(z, 1 - y, c), None)
-    send(vv_ref, me, index(z, y, 1 - c), None)
+    for h in range(CHUNKS):
+        send(vv_ref, me, h, index(up, y, c), up_ok)
+        send(vv_ref, me, h, index(down, y, c), down_ok)
+        if ny == 2:
+            send(vv_ref, me, h, index(z, 1 - y, c), None)
+        send(vv_ref, me, h, index(z, y, 1 - c), None)
 
     def one_partial(s, carry):
         p = perm_ref[s]
@@ -90,17 +99,19 @@
     inbuf[here, :] = part[here, :]
 
     def z_step(k):
-        for zz, okay, nxt, nxt_ok in ((z - k, z >= k, up, up_ok), (z + k, z + k < nz, down, down_ok)):
-            zs = jnp.clip(zz, 0, nz - 1)
-            shard = index(zs, y, c)
-            arrived(shard, okay)
-            src = gbuf.at[shard]
-            send(src, shard, index(nxt, y, c), jnp.logical_and(okay, nxt_ok))
-            if ny == 2:
-                send(src, shard, index(z, 1 - y, c), okay)
-            send(src, shard, index(z, y, 1 - c), okay)
-
-    z_step(1)
+        for h in range(CHUNKS):
+            for zz, okay, nxt, nxt_ok in ((z - k, z >= k, up, up_ok), (z + k, z + k < nz, down, down_ok)):
+                zs = jnp.clip(zz, 0, nz - 1)
+                shard = index(zs, y, c)
+                arrived(shard, h, okay)
+                src = gbuf.at[shard]
+                send(src, shard, h, index(nxt, y, c), jnp.logical_and(okay, nxt_ok))
+                if ny == 2:
+                    send(src, shard, h, index(z, 1 - y, c), okay)
+                send(src, shard, h, index(z, y, 1 - c), okay)
+
+    for k in range(1, nz):
+        z_step(k)
 
     for cp in go:
         cp.wait_recv()
@@ -123,9 +134,6 @@
         cp.start()
         ret.append(cp)
     chosen_ref[here, :] = back[here, :]
-
-    for k in range(2, nz):
-        z_step(k)
 
     def relayout(lo, hi, m):
         if rows_dev != 8:
@@ -151,7 +159,8 @@
     gbuf[me] = vv_ref[...]
     for k in range(nz):
         zz = (z + k) % nz
-        arrived(index(zz, y, 1 - c))
+        for h in range(CHUNKS):
+            arrived(index(zz, y, 1 - c), h)
         chip(zz, y)
     if ny == 2:
         order = [(z, None)]
@@ -159,13 +168,15 @@
             order += [(z - k, z >= k), (z + k, z + k < nz)]
         for zz, cond in order:
             shard = index(jnp.clip(zz, 0, nz - 1), 1 - y, c)
-            arrived(shard, cond)
-            send(gbuf.at[shard], shard, index(z, y, 1 - c), cond)
+            for h in range(CHUNKS):
+                arrived(shard, h, cond)
+                send(gbuf.at[shard], shard, h, index(z, y, 1 - c), cond)
         for zz, cond in order:
             zc = jnp.clip(zz, 0, nz - 1)
 
             def finish(zc=zc):
-                arrived(index(zc, 1 - y, 1 - c))
+                for h in range(CHUNKS):
+                    arrived(index(zc, 1 - y, 1 - c), h)
                 chip(zc, 1 - y)
 
             if cond is None:
@@ -260,8 +271,8 @@
             pltpu.VMEM(flat, BF16),
             pltpu.VMEM(flat, BF16),
             pltpu.VMEM(flat, BF16),
-            dma((sends,)),
-            dma((n,)),
+            dma((sends * CHUNKS,)),
+            dma((n * CHUNKS,)),
             dma((n,)),
             dma((n,)),
             dma((n,)),

time: 91.9 us -> 87.8 us (0.955)
  Pallas kernels: 84.9 us -> 80.7 us
    pallas_call x1, Pallas kernels: 57.4 us -> 53.3 us  [body(): pl.pallas_call(functools.partial(comm_kernel, n, cap, fit_count), out_sha...]
where the time goes in v2:
time: 87.8 us; the launch traced here: 87.5 us
  Pallas kernels  80.7 us (92%)
  local copies, waits for them, and re-layouts  5.71 us (7%)
  other arithmetic  0.95 us (1%)
    pallas_call x1, Pallas kernels, body(): pl.pallas_call(functools.partial(comm_kernel, n, cap, fit_count), out_sha...  53.3 us
    pallas_call x1, Pallas kernels, body(): pl.pallas_call(ladder_kernel, out_shape=jax.ShapeDtypeStruct(amplitudes.s...  27.4 us
    unnamed x6, local copies, waits for them, and re-layouts  2.48 us

profile of v2, /device:TPU:1, one launch (start us, length us, event | category | flops | bytes accessed | tf_op | source)
XLA Modules:
  0.0 87.5 jit_solution(603949345545137572)
XLA Ops:
  0.0 0.8 constant_dynamic-slice_fusion
  0.8 0.2 convert_reduce_fusion.1
  1.0 0.1 select_reduce_fusion.1
  1.1 0.8 reshape.183
  1.9 0.4 convert_reduce_fusion
  2.3 0.1 select_reduce_fusion
  2.5 0.1 copy.9
  2.6 0.1 mul.70
  2.7 0.1 iota_add_fusion
  2.7 0.1 add.102.code_row_ref
  2.8 1.1 %copy.8 = bf16[12,16,8,128]{3,2,1,0:T(8,128)(2,1)S(1)} copy(bf16[12,16,8,128]{3,1,2,0:T(8,128)(2,1)} %bitcast.48) | data formatting | bytes 786432 | tf_op jit(solution)/shard_map/transpose | solution.py:254
  3.9 0.3 add.103.code_col_ref
  4.2 0.0 copy-start
  4.3 1.6 %copy-done = bf16[64,128,128]{2,1,0:T(8,128)(2,1)S(1)} copy-done((bf16[64,128,128]{2,1,0:T(8,128)(2,1)S(1)}, bf16[64,128,128]{2,1,0:T(8,128)(2,1)}, u32[]{:S(2)}) %copy-start) | copy-done | bytes 2097176
  5.8 0.0 copy-start.2
  5.8 0.9 %copy-done.2 = bf16[2,12,16,128]{3,2,1,0:T(8,128)(2,1)S(1)} copy-done((bf16[2,12,16,128]{3,2,1,0:T(8,128)(2,1)S(1)}, bf16[2,12,16,128]{3,2,1,0:T(8,128)(2,1)}, u32[]{:S(2)}) %copy-start.2) | copy-done | bytes 98328
  6.7 0.0 copy-start.1
  6.7 53.3 %gather_and_totals.1 = (bf16[12,16,128,128]{3,2,1,0:T(8,128)(2,1)}, bf16[1024,128]{1,0:T(8,128)(2,1)S(1)}) custom-call(s32[64]{0:T(128)S(1)} %get-tuple-element.10.perm_ref, s32[64]{0:T(128)S(1)} %get-tuple-element.9.row_ref, bf16[12,8,16,128]{3,2,1,0:T(8,128)(2,1)S(1)} %bitcast.44, bf16[64,128,128]{2,1,0:T(8,128)(2,1)S(1)} %copy-done, ...), custom_call_target="tpu_custom_call" | custom-call | tf_op jit(solution)/shard_map/gather_and_totals/pallas_call | solution.py:264
  60.0 0.0 copy-done.1
  60.0 27.4 %ladder.1 = bf16[64,128,128]{2,1,0:T(8,128)(2,1)} custom-call(s32[64]{0:T(128)S(1)} %get-tuple-element.15.a_ids, s32[64]{0:T(128)S(1)} %get-tuple-element.14.b_ids, s32[64]{0:T(128)S(1)} %get-tuple-element.17.fit_ids, s32[64]{0:T(128)S(1)} %multiply_add_fusion.slots, bf16[12,16,128,128]{3,2,1,0:T(8,128)(2,1)} %get-tuple-element.7.v_ref, ...), custom_call_target="tpu_custom_call" | custom-call | flops 8589934592 | bytes 12582912 | tf_op jit(solution)/shard_map/ladder/pallas_call | solution.py:289
  (8 shorter events, 0.1 us)
Async XLA Ops:
  4.2 1.6 %copy-start = (bf16[64,128,128]{2,1,0:T(8,128)(2,1)S(1)}, bf16[64,128,128]{2,1,0:T(8,128)(2,1)}, u32[]{:S(2)}) copy-start(bf16[64,128,128]{2,1,0:T(8,128)(2,1)} %amp_ref.3) | copy-start | bytes 6291460
  5.8 0.9 %copy-start.2 = (bf16[2,12,16,128]{3,2,1,0:T(8,128)(2,1)S(1)}, bf16[2,12,16,128]{3,2,1,0:T(8,128)(2,1)}, u32[]{:S(2)}) copy-start(bf16[2,12,16,128]{3,2,1,0:T(8,128)(2,1)} %param.7) | copy-start | bytes 294916
  6.7 53.3 %copy-start.1 = (bf16[64,128,128]{2,1,0:T(8,128)(2,1)S(1)}, bf16[64,128,128]{2,1,0:T(8,128)(2,1)}, u32[]{:S(2)}) copy-start(bf16[64,128,128]{2,1,0:T(8,128)(2,1)} %amp_ref.3) | copy-start | bytes 6291460

commit v3 on v2

--- a/solution.py
+++ b/solution.py
@@ -217,7 +217,7 @@
         out_ref[p] = (acc + cyc.astype(F32)).astype(BF16)
         return carry
 
-    lax.fori_loop(0, tiles, one, 0, unroll=2)
+    lax.fori_loop(0, tiles, one, 0, unroll=4)
 
 
 def body(amplitudes, pair_tiles, fit_vv, fit_ov):
@@ -279,7 +279,7 @@
             dma((n,)),
         ],
         compiler_params=pltpu.CompilerParams(
-            collective_id=0, has_side_effects=True, vmem_limit_bytes=48 * 2**20),
+            collective_id=0, has_side_effects=True, vmem_limit_bytes=24 * 2**20),
         name="gather_and_totals",
     )(perm, slot_fit, own, amplitudes, fits, code[:, None], code[None, :])
     if rows_dev != 8:
@@ -291,7 +291,7 @@
         out_shape=jax.ShapeDtypeStruct(amplitudes.shape, BF16),
         in_specs=[smem, smem, smem, smem, vmem, vmem, vmem, vmem],
         out_specs=vmem,
-        compiler_params=pltpu.CompilerParams(vmem_limit_bytes=48 * 2**20),
+        compiler_params=pltpu.CompilerParams(vmem_limit_bytes=24 * 2**20),
         cost_estimate=pl.CostEstimate(flops=flops, bytes_accessed=12 * 2**20, transcendentals=0),
         name="ladder",
     )(tile_a, tile_b, fit_ids, slot, whole, amplitudes, fits, chosen)

time: 87.8 us -> 80.3 us (0.915)
  Pallas kernels: 80.7 us -> 73.2 us
    pallas_call x1, Pallas kernels: 27.4 us -> 22.6 us  [body(): pl.pallas_call(ladder_kernel, out_shape=jax.ShapeDtypeStruct(amplitudes.s...]
    pallas_call x1, Pallas kernels: 53.3 us -> 50.6 us  [body(): pl.pallas_call(functools.partial(comm_kernel, n, cap, fit_count), out_sha...]
where the time goes in v3:
time: 80.3 us; the launch traced here: 80 us
  Pallas kernels  73.2 us (91%)
  local copies, waits for them, and re-layouts  5.71 us (7%)
  other arithmetic  0.95 us (1%)
    pallas_call x1, Pallas kernels, body(): pl.pallas_call(functools.partial(comm_kernel, n, cap, fit_count), out_sha...  50.6 us
    pallas_call x1, Pallas kernels, body(): pl.pallas_call(ladder_kernel, out_shape=jax.ShapeDtypeStruct(amplitudes.s...  22.6 us
    unnamed x6, local copies, waits for them, and re-layouts  2.48 us

profile of v3, /device:TPU:1, one launch (start us, length us, event | category | flops | bytes accessed | tf_op | source)
XLA Modules:
  0.0 80.0 jit_solution(17685311499505611307)
XLA Ops:
  0.0 0.8 constant_dynamic-slice_fusion
  0.8 0.2 convert_reduce_fusion.1
  1.0 0.1 select_reduce_fusion.1
  1.1 0.8 %reshape.183 = s32[16,64,4]{1,0,2:T(8,128)S(1)} reshape(s32[1024,4]{0,1:T(4,128)} %param.5) | data formatting | bytes 32768 | tf_op jit(solution)/shard_map/reshape | solution.py:243
  1.9 0.4 convert_reduce_fusion
  2.3 0.1 select_reduce_fusion
  2.5 0.1 copy.9
  2.6 0.1 mul.70
  2.7 0.1 iota_add_fusion
  2.7 0.1 add.102.code_row_ref
  2.8 1.1 %copy.8 = bf16[12,16,8,128]{3,2,1,0:T(8,128)(2,1)S(1)} copy(bf16[12,16,8,128]{3,1,2,0:T(8,128)(2,1)} %bitcast.48) | data formatting | bytes 786432 | tf_op jit(solution)/shard_map/transpose | solution.py:254
  3.9 0.3 add.103.code_col_ref
  4.2 0.0 copy-start
  4.3 1.6 %copy-done = bf16[64,128,128]{2,1,0:T(8,128)(2,1)S(1)} copy-done((bf16[64,128,128]{2,1,0:T(8,128)(2,1)S(1)}, bf16[64,128,128]{2,1,0:T(8,128)(2,1)}, u32[]{:S(2)}) %copy-start) | copy-done | bytes 2097176
  5.8 0.0 copy-start.2
  5.8 0.9 %copy-done.2 = bf16[2,12,16,128]{3,2,1,0:T(8,128)(2,1)S(1)} copy-done((bf16[2,12,16,128]{3,2,1,0:T(8,128)(2,1)S(1)}, bf16[2,12,16,128]{3,2,1,0:T(8,128)(2,1)}, u32[]{:S(2)}) %copy-start.2) | copy-done | bytes 98328
  6.7 0.0 copy-start.1
  6.7 50.6 %gather_and_totals.1 = (bf16[12,16,128,128]{3,2,1,0:T(8,128)(2,1)S(1)}, bf16[1024,128]{1,0:T(8,128)(2,1)S(1)}) custom-call(s32[64]{0:T(128)S(1)} %get-tuple-element.10.perm_ref, s32[64]{0:T(128)S(1)} %get-tuple-element.9.row_ref, bf16[12,8,16,128]{3,2,1,0:T(8,128)(2,1)S(1)} %bitcast.44, bf16[64,128,128]{2,1,0:T(8,128)(2,1)S(1)} %copy-done, ...), custom_call_target="tpu_custom_call" | custom-call | tf_op jit(solution)/shard_map/gather_and_totals/pallas_call | solution.py:264
  57.4 0.0 copy-done.1
  57.4 22.6 %ladder.1 = bf16[64,128,128]{2,1,0:T(8,128)(2,1)} custom-call(s32[64]{0:T(128)S(1)} %get-tuple-element.15.a_ids, s32[64]{0:T(128)S(1)} %get-tuple-element.14.b_ids, s32[64]{0:T(128)S(1)} %get-tuple-element.17.fit_ids, s32[64]{0:T(128)S(1)} %multiply_add_fusion.slots, bf16[12,16,128,128]{3,2,1,0:T(8,128)(2,1)S(1)} %get-tuple-element.7.v_ref, ...), custom_call_target="tpu_custom_call" | custom-call | flops 8589934592 | bytes 12582912 | tf_op jit(solution)/shard_map/ladder/pallas_call | solution.py:289
  (8 shorter events, 0.1 us)
Async XLA Ops:
  4.2 1.6 %copy-start = (bf16[64,128,128]{2,1,0:T(8,128)(2,1)S(1)}, bf16[64,128,128]{2,1,0:T(8,128)(2,1)}, u32[]{:S(2)}) copy-start(bf16[64,128,128]{2,1,0:T(8,128)(2,1)} %amp_ref.3) | copy-start | bytes 6291460
  5.8 0.9 %copy-start.2 = (bf16[2,12,16,128]{3,2,1,0:T(8,128)(2,1)S(1)}, bf16[2,12,16,128]{3,2,1,0:T(8,128)(2,1)}, u32[]{:S(2)}) copy-start(bf16[2,12,16,128]{3,2,1,0:T(8,128)(2,1)} %param.7) | copy-start | bytes 294916
  6.7 50.6 %copy-start.1 = (bf16[64,128,128]{2,1,0:T(8,128)(2,1)S(1)}, bf16[64,128,128]{2,1,0:T(8,128)(2,1)}, u32[]{:S(2)}) copy-start(bf16[64,128,128]{2,1,0:T(8,128)(2,1)} %amp_ref.3) | copy-start | bytes 6291460

commit v4 on v3

--- a/solution.py
+++ b/solution.py
@@ -11,7 +11,7 @@
 BF16 = jnp.bfloat16
 
 
-CHUNKS = 4
+CHUNKS = 2
 
 
 def grid_of(n):
@@ -217,7 +217,7 @@
         out_ref[p] = (acc + cyc.astype(F32)).astype(BF16)
         return carry
 
-    lax.fori_loop(0, tiles, one, 0, unroll=4)
+    lax.fori_loop(0, tiles, one, 0, unroll=8)
 
 
 def body(amplitudes, pair_tiles, fit_vv, fit_ov):

time: 80.3 us -> 78.3 us (0.975)
  Pallas kernels: 73.2 us -> 71.3 us
    pallas_call x1, Pallas kernels: 22.6 us -> 21.4 us  [body(): pl.pallas_call(ladder_kernel, out_shape=jax.ShapeDtypeStruct(amplitudes.s...]
where the time goes in v4:
time: 78.3 us; the launch traced here: 78 us
  Pallas kernels  71.3 us (91%)
  local copies, waits for them, and re-layouts  5.71 us (7%)
  other arithmetic  0.95 us (1%)
    pallas_call x1, Pallas kernels, body(): pl.pallas_call(functools.partial(comm_kernel, n, cap, fit_count), out_sha...  49.9 us
    pallas_call x1, Pallas kernels, body(): pl.pallas_call(ladder_kernel, out_shape=jax.ShapeDtypeStruct(amplitudes.s...  21.4 us
    unnamed x6, local copies, waits for them, and re-layouts  2.48 us

profile of v4, /device:TPU:1, one launch (start us, length us, event | category | flops | bytes accessed | tf_op | source)
XLA Modules:
  0.0 78.0 jit_solution(8631151812228417697)
XLA Ops:
  0.0 0.8 constant_dynamic-slice_fusion
  0.8 0.2 convert_reduce_fusion.1
  1.0 0.1 select_reduce_fusion.1
  1.1 0.8 %reshape.183 = s32[16,64,4]{1,0,2:T(8,128)S(1)} reshape(s32[1024,4]{0,1:T(4,128)} %param.5) | data formatting | bytes 32768 | tf_op jit(solution)/shard_map/reshape | solution.py:243
  1.9 0.4 convert_reduce_fusion
  2.3 0.1 select_reduce_fusion
  2.5 0.1 copy.9
  2.6 0.1 mul.70
  2.7 0.1 iota_add_fusion
  2.7 0.1 add.102.code_row_ref
  2.8 1.1 %copy.8 = bf16[12,16,8,128]{3,2,1,0:T(8,128)(2,1)S(1)} copy(bf16[12,16,8,128]{3,1,2,0:T(8,128)(2,1)} %bitcast.48) | data formatting | bytes 786432 | tf_op jit(solution)/shard_map/transpose | solution.py:254
  3.9 0.3 add.103.code_col_ref
  4.2 0.0 copy-start
  4.3 1.6 %copy-done = bf16[64,128,128]{2,1,0:T(8,128)(2,1)S(1)} copy-done((bf16[64,128,128]{2,1,0:T(8,128)(2,1)S(1)}, bf16[64,128,128]{2,1,0:T(8,128)(2,1)}, u32[]{:S(2)}) %copy-start) | copy-done | bytes 2097176
  5.8 0.0 copy-start.2
  5.8 0.9 %copy-done.2 = bf16[2,12,16,128]{3,2,1,0:T(8,128)(2,1)S(1)} copy-done((bf16[2,12,16,128]{3,2,1,0:T(8,128)(2,1)S(1)}, bf16[2,12,16,128]{3,2,1,0:T(8,128)(2,1)}, u32[]{:S(2)}) %copy-start.2) | copy-done | bytes 98328
  6.7 0.0 copy-start.1
  6.7 49.9 %gather_and_totals.1 = (bf16[12,16,128,128]{3,2,1,0:T(8,128)(2,1)S(1)}, bf16[1024,128]{1,0:T(8,128)(2,1)S(1)}) custom-call(s32[64]{0:T(128)S(1)} %get-tuple-element.10.perm_ref, s32[64]{0:T(128)S(1)} %get-tuple-element.9.row_ref, bf16[12,8,16,128]{3,2,1,0:T(8,128)(2,1)S(1)} %bitcast.44, bf16[64,128,128]{2,1,0:T(8,128)(2,1)S(1)} %copy-done, ...), custom_call_target="tpu_custom_call" | custom-call | tf_op jit(solution)/shard_map/gather_and_totals/pallas_call | solution.py:264
  56.6 0.0 copy-done.1
  56.6 21.4 %ladder.1 = bf16[64,128,128]{2,1,0:T(8,128)(2,1)} custom-call(s32[64]{0:T(128)S(1)} %get-tuple-element.15.a_ids, s32[64]{0:T(128)S(1)} %get-tuple-element.14.b_ids, s32[64]{0:T(128)S(1)} %get-tuple-element.17.fit_ids, s32[64]{0:T(128)S(1)} %multiply_add_fusion.slots, bf16[12,16,128,128]{3,2,1,0:T(8,128)(2,1)S(1)} %get-tuple-element.7.v_ref, ...), custom_call_target="tpu_custom_call" | custom-call | flops 8589934592 | bytes 12582912 | tf_op jit(solution)/shard_map/ladder/pallas_call | solution.py:289
  (8 shorter events, 0.1 us)
Async XLA Ops:
  4.2 1.6 %copy-start = (bf16[64,128,128]{2,1,0:T(8,128)(2,1)S(1)}, bf16[64,128,128]{2,1,0:T(8,128)(2,1)}, u32[]{:S(2)}) copy-start(bf16[64,128,128]{2,1,0:T(8,128)(2,1)} %amp_ref.3) | copy-start | bytes 6291460
  5.8 0.9 %copy-start.2 = (bf16[2,12,16,128]{3,2,1,0:T(8,128)(2,1)S(1)}, bf16[2,12,16,128]{3,2,1,0:T(8,128)(2,1)}, u32[]{:S(2)}) copy-start(bf16[2,12,16,128]{3,2,1,0:T(8,128)(2,1)} %param.7) | copy-start | bytes 294916
  6.7 49.9 %copy-start.1 = (bf16[64,128,128]{2,1,0:T(8,128)(2,1)S(1)}, bf16[64,128,128]{2,1,0:T(8,128)(2,1)}, u32[]{:S(2)}) copy-start(bf16[64,128,128]{2,1,0:T(8,128)(2,1)} %amp_ref.3) | copy-start | bytes 6291460

commit v5 on v4

--- a/solution.py
+++ b/solution.py
@@ -217,7 +217,7 @@
         out_ref[p] = (acc + cyc.astype(F32)).astype(BF16)
         return carry
 
-    lax.fori_loop(0, tiles, one, 0, unroll=8)
+    lax.fori_loop(0, tiles, one, 0, unroll=16)
 
 
 def body(amplitudes, pair_tiles, fit_vv, fit_ov):

time: 78.3 us -> 77.7 us (level)
  no operation moved by 1% of the time
where the time goes in v5:
time: 77.7 us; the launch traced here: 77.4 us
  Pallas kernels  70.6 us (91%)
  local copies, waits for them, and re-layouts  5.71 us (7%)
  other arithmetic  0.95 us (1%)
    pallas_call x1, Pallas kernels, body(): pl.pallas_call(functools.partial(comm_kernel, n, cap, fit_count), out_sha...  49.9 us
    pallas_call x1, Pallas kernels, body(): pl.pallas_call(ladder_kernel, out_shape=jax.ShapeDtypeStruct(amplitudes.s...  20.7 us
    unnamed x6, local copies, waits for them, and re-layouts  2.48 us

profile of v5, /device:TPU:1, one launch (start us, length us, event | category | flops | bytes accessed | tf_op | source)
XLA Modules:
  0.0 77.4 jit_solution(12401733243821858018)
XLA Ops:
  0.0 0.8 constant_dynamic-slice_fusion
  0.8 0.2 convert_reduce_fusion.1
  1.0 0.1 select_reduce_fusion.1
  1.1 0.8 %reshape.183 = s32[16,64,4]{1,0,2:T(8,128)S(1)} reshape(s32[1024,4]{0,1:T(4,128)} %param.5) | data formatting | bytes 32768 | tf_op jit(solution)/shard_map/reshape | solution.py:243
  1.9 0.4 convert_reduce_fusion
  2.3 0.1 select_reduce_fusion
  2.5 0.1 copy.9
  2.6 0.1 mul.70
  2.7 0.1 iota_add_fusion
  2.7 0.1 add.102.code_row_ref
  2.8 1.1 %copy.8 = bf16[12,16,8,128]{3,2,1,0:T(8,128)(2,1)S(1)} copy(bf16[12,16,8,128]{3,1,2,0:T(8,128)(2,1)} %bitcast.48) | data formatting | bytes 786432 | tf_op jit(solution)/shard_map/transpose | solution.py:254
  3.9 0.3 add.103.code_col_ref
  4.2 0.0 copy-start
  4.3 1.6 %copy-done = bf16[64,128,128]{2,1,0:T(8,128)(2,1)S(1)} copy-done((bf16[64,128,128]{2,1,0:T(8,128)(2,1)S(1)}, bf16[64,128,128]{2,1,0:T(8,128)(2,1)}, u32[]{:S(2)}) %copy-start) | copy-done | bytes 2097176
  5.8 0.0 copy-start.2
  5.8 0.9 %copy-done.2 = bf16[2,12,16,128]{3,2,1,0:T(8,128)(2,1)S(1)} copy-done((bf16[2,12,16,128]{3,2,1,0:T(8,128)(2,1)S(1)}, bf16[2,12,16,128]{3,2,1,0:T(8,128)(2,1)}, u32[]{:S(2)}) %copy-start.2) | copy-done | bytes 98328
  6.7 0.0 copy-start.1
  6.7 49.9 %gather_and_totals.1 = (bf16[12,16,128,128]{3,2,1,0:T(8,128)(2,1)S(1)}, bf16[1024,128]{1,0:T(8,128)(2,1)S(1)}) custom-call(s32[64]{0:T(128)S(1)} %get-tuple-element.10.perm_ref, s32[64]{0:T(128)S(1)} %get-tuple-element.9.row_ref, bf16[12,8,16,128]{3,2,1,0:T(8,128)(2,1)S(1)} %bitcast.44, bf16[64,128,128]{2,1,0:T(8,128)(2,1)S(1)} %copy-done, ...), custom_call_target="tpu_custom_call" | custom-call | tf_op jit(solution)/shard_map/gather_and_totals/pallas_call | solution.py:264
  56.6 0.0 copy-done.1
  56.6 20.7 %ladder.1 = bf16[64,128,128]{2,1,0:T(8,128)(2,1)} custom-call(s32[64]{0:T(128)S(1)} %get-tuple-element.15.a_ids, s32[64]{0:T(128)S(1)} %get-tuple-element.14.b_ids, s32[64]{0:T(128)S(1)} %get-tuple-element.17.fit_ids, s32[64]{0:T(128)S(1)} %multiply_add_fusion.slots, bf16[12,16,128,128]{3,2,1,0:T(8,128)(2,1)S(1)} %get-tuple-element.7.v_ref, ...), custom_call_target="tpu_custom_call" | custom-call | flops 8589934592 | bytes 12582912 | tf_op jit(solution)/shard_map/ladder/pallas_call | solution.py:289
  (8 shorter events, 0.1 us)
Async XLA Ops:
  4.2 1.6 %copy-start = (bf16[64,128,128]{2,1,0:T(8,128)(2,1)S(1)}, bf16[64,128,128]{2,1,0:T(8,128)(2,1)}, u32[]{:S(2)}) copy-start(bf16[64,128,128]{2,1,0:T(8,128)(2,1)} %amp_ref.3) | copy-start | bytes 6291460
  5.8 0.9 %copy-start.2 = (bf16[2,12,16,128]{3,2,1,0:T(8,128)(2,1)S(1)}, bf16[2,12,16,128]{3,2,1,0:T(8,128)(2,1)}, u32[]{:S(2)}) copy-start(bf16[2,12,16,128]{3,2,1,0:T(8,128)(2,1)} %param.7) | copy-start | bytes 294916
  6.7 49.9 %copy-start.1 = (bf16[64,128,128]{2,1,0:T(8,128)(2,1)S(1)}, bf16[64,128,128]{2,1,0:T(8,128)(2,1)}, u32[]{:S(2)}) copy-start(bf16[64,128,128]{2,1,0:T(8,128)(2,1)} %amp_ref.3) | copy-start | bytes 6291460
